TPU v7x, 512 devices: a whole 4x4x16 slice. The times are simulated.
512 devices in a mesh: dp: 64 (over x_hi, z, core), space: 8 (over x_lo, y).
Axes of the slice: x: 4 (x_hi: 2, x_lo: 2; x = x_hi * 2 + x_lo), y: 4, z: 16, core: 2. Of those that a mesh axis runs over, the one named last changes fastest.
Arguments:
- features: bfloat16 [131072, 128], P(('dp', 'space')), may hold values from -6 to 6
- teacher: bfloat16 [131072, 256], P(('dp', 'space')), may hold values from -6 to 6
- weight: bfloat16 [3456, 256], replicated, may hold values from -0.109375 to 0.109375
- neighbours: int32 [131072, 27], P(('dp', 'space')), may hold values from -1 to 383, as said below
- counts: int32 [512], replicated, may hold values from 128 to 256, as said below
Outputs:
- grad_input: bfloat16 [131072, 128], P(('dp', 'space'))
- grad_weight: float32 [3456, 256], P('dp')
- loss: float32 [], replicated
Inputs may be any that keep to these rules, and one draw needn't show every extreme that they name: `neighbours`: window positions below 64 lie on the device one lower along space, positions 320 and up on the device one higher, and every named slot is valid and of the same scene. Offset 13 of a valid site names the site itself; padding slots have -1 everywhere. `counts`: some device has all 256 slots valid.
All inputs are finite; a program needn't handle non-finite values.
Results may differ from a plain program's by a relative error of at most 0.0075.
Values may be sent and summed in bfloat16 or wider, within the bound.
A program may use at most 64 MiB of HBM per device.

v0:
```python
import jax
import jax.numpy as jnp
from jax import lax
from jax.sharding import PartitionSpec as P


def padded_2(x, sides, width):
    for axis, dim in sides:
        size, length = (lax.axis_size(axis), x.shape[dim])
        up = [(i, (i + 1) % size) for i in range(size - 1)]
        down = [(j, i) for i, j in up]
        last = lax.slice_in_dim(x, length - width, length, axis=dim)
        first = lax.slice_in_dim(x, 0, width, axis=dim)
        before = lax.ppermute(last, axis, up)
        after = lax.ppermute(first, axis, down)
        x = jnp.concatenate([before, x, after], axis=dim)
    return x


def shifted(value, axis, steps):
    count = lax.axis_size(axis)
    first, last = (max(0, -steps), min(count, count - steps))
    return lax.ppermute(value, axis, [(source, source + steps) for source in range(first, last)])


def shards(features, teacher, weight, neighbours, counts):
    rows = features.shape[0]
    chans = features.shape[1]
    outs_width = teacher.shape[1]
    offsets = neighbours.shape[1]
    edge = rows // 4
    n_space = lax.axis_size("space")
    device = lax.axis_index("dp") * n_space + lax.axis_index("space")
    padded = padded_2(features, (("space", 0),), edge)
    padded = jnp.concatenate([padded, jnp.zeros((1, chans), jnp.bfloat16)], axis=0)
    index = jnp.where(neighbours < 0, rows + 2 * edge, neighbours)
    gathered = jnp.take(padded, index, axis=0).reshape(rows, offsets * chans)
    z_out = jnp.dot(gathered, weight, preferred_element_type=jnp.float32)
    limit = lax.dynamic_slice_in_dim(counts, device, 1)[0]
    slots = jnp.arange(rows, dtype=jnp.int32)
    valid = (slots < limit - edge) | (slots >= rows - edge)
    diff = jnp.where(valid[:, None], z_out - teacher.astype(jnp.float32), jnp.float32(0.0))
    partial_sq = jnp.sum(diff * diff)
    grad_z = (diff / outs_width).astype(jnp.bfloat16)
    local_grad = lax.dot_general(
        gathered, grad_z, (((0,), (0,)), ((), ())), preferred_element_type=jnp.float32
    )
    scene_total = lax.psum(local_grad.astype(jnp.bfloat16), "space").astype(jnp.float32)
    grad_weight = lax.psum_scatter(scene_total, "dp", scatter_dimension=0, tiled=True)
    grad_g = jnp.dot(grad_z, weight.T, preferred_element_type=jnp.float32)
    spread = jax.ops.segment_sum(
        grad_g.reshape(rows * offsets, chans), index.reshape(-1), num_segments=rows + 2 * edge + 1
    )
    below = spread[:edge]
    above = spread[edge + rows : rows + 2 * edge]
    own = spread[edge : edge + rows]
    from_upper = shifted(below.astype(jnp.bfloat16), "space", -1).astype(below.dtype)
    from_lower = shifted(above.astype(jnp.bfloat16), "space", 1).astype(above.dtype)
    own = jnp.concatenate(
        [own[:edge] + from_lower, own[edge : rows - edge], own[rows - edge :] + from_upper], axis=0
    )
    grad_input = own.astype(jnp.bfloat16)
    total_sq = lax.psum(partial_sq, ("dp", "space"))
    loss = 0.5 * total_sq / (outs_width * jnp.sum(counts).astype(jnp.float32))
    return (grad_input, grad_weight, loss)


def solution(mesh):
    placed = (
        P(("dp", "space"), None),
        P(("dp", "space"), None),
        P(),
        P(("dp", "space"), None),
        P(),
    )
    return jax.shard_map(
        shards,
        mesh=mesh,
        in_specs=placed,
        out_specs=(P(("dp", "space"), None), P("dp", None), P()),
        check_vma=False,
    )
```

profile of v0, /device:TPU:4, one launch (start us, length us, event | category | flops | bytes accessed | tf_op | source)
XLA Modules:
  0.0 403.3 jit_solution(1992243658142156235)
XLA Ops:
  7.2 0.9 fusion.10
  8.1 3.5 collective-permute-start
  11.6 1.3 collective-permute-start.1
  12.9 0.8 compare_and_fusion
  13.6 1.4 compare_select_fusion
  15.4 1.3 dynamic_slice.3
  17.5 1.0 maximum_maximum_fusion
  18.4 14.7 %gather_fusion = bf16[6912,128]{1,0:T(8,128)(2,1)} fusion(bf16[385,128]{1,0:T(8,128)(2,1)S(1)} %maximum_maximum_fusion, s32[7168]{0:T(1024)S(1)} %pad_clamp_fusion), kind=kCustom, calls=%fused_computation | custom fusion | bytes 3566592 | tf_op jit(solution)/shard_map/jit(_take)/gather | solution.py:37
  33.1 3.8 reshape.30
  37.0 4.4 %broadcast_select_fusion = bf16[256,27,128]{2,1,0:T(8,128)(2,1)} fusion(bf16[256,27,128]{2,1,0:T(8,128)(2,1)} %reshape.30, pred[256,27]{1,0:T(8,128)(4,1)S(1)} %copy.14), kind=kLoop, calls=%fused_computation.3 | loop fusion | flops 884736 | bytes 3545856 | tf_op jit(solution)/shard_map/jit(_take)/select_n | solution.py:37
  41.3 3.3 copy.16
  44.7 2.2 multiply_reduce_fusion
  46.9 0.7 copy-done.1
  47.6 1.9 convolution_convert_fusion
  49.5 0.9 copy.13
  50.6 2.4 fusion.4
  53.0 4.6 %reshape.41 = f32[6912,128]{1,0:T(8,128)} reshape(f32[256,3456]{1,0:T(8,128)} %fusion.4) | data formatting | bytes 7077888 | tf_op jit(solution)/shard_map/reshape | solution.py:52
  57.6 42.8 %scatter_custom_fusion = f32[385,128]{1,0:T(8,128)S(1)} fusion(s32[6912]{0:T(1024)S(1)} %reshape.39, f32[6912,128]{1,0:T(8,128)} %reshape.41, f32[]{:T(128)} %constant.16.clone.1), kind=kCustom, calls=%fused_computation.9 | custom fusion | flops 884736 | bytes 197632 | tf_op jit(solution)/shard_map/scatter-add | solution.py:51
  100.5 2.3 collective-permute-start.2
  102.8 1.3 collective-permute-start.3
  104.1 0.6 reduce_sum.19
  105.4 1.3 dynamic-slice.4
  107.3 115.6 %psum.15 = f32[]{:T(128)} all-reduce(f32[]{:T(128)} %get-tuple-element.11), channel_id=1, replica_groups=mesh['dp'=64,'space'=8] {'dp','space'}, use_global_device_ids=true, to_apply=%region_4.5 | all-reduce | flops 1 | bytes 8 | tf_op jit(solution)/shard_map/psum | solution.py:63
  223.7 3.5 convert_element_type.29
  227.2 153.1 %fusion = f32[56,256]{1,0:T(8,128)S(1)} fusion(f32[3456,256]{1,0:T(8,128)} %convert_element_type.29), kind=kCustom, calls=%all-reduce-scatter | all-reduce-scatter fusion | flops 917505 | bytes 3598336
  380.3 1.9 collective-permute-start.5
  382.2 1.9 collective-permute-start.4
  384.1 1.9 collective-permute-start.6
  386.0 0.6 pad_maximum_fusion
  386.7 7.6 %collective-permute-done.6 = f32[14,256]{1,0:T(8,128)S(1)} collective-permute-done((f32[14,256]{1,0:T(8,128)S(1)}, f32[14,256]{1,0:T(8,128)S(1)}, u32[]{:S(2)}, u32[]{:S(2)}) %collective-permute-start.6) | collective-permute-done | bytes 14368
  394.2 0.5 concatenate.9
  394.7 0.6 constant_dynamic-slice_fusion
  (28 shorter events, 0.8 us)
Async XLA Ops:
  7.2 37.5 %copy-start = (bf16[3456,256]{1,0:T(8,128)(2,1)S(1)}, bf16[3456,256]{1,0:T(8,128)(2,1)}, u32[]{:S(2)}) copy-start(bf16[3456,256]{1,0:T(8,128)(2,1)} %param.7) | copy-start | bytes 5308420
  7.2 216.5 %all-reduce.4.cloned.1.call-start = ((), (), s32[]{:S(2)}) async-start(), calls=%async_computation | async-start | bytes 3538944 | tf_op jit(solution)/shard_map/psum | solution.py:48
  8.1 9.4 %collective-permute-start = (bf16[64,128]{1,0:T(8,128)(2,1)S(1)}, bf16[64,128]{1,0:T(8,128)(2,1)S(1)}, u32[]{:S(2)}, u32[]{:S(2)}) collective-permute-start(bf16[64,128]{1,0:T(8,128)(2,1)S(1)} %get-tuple-element.7), channel_id=1, source_target_pairs={{0,1},{1,2},{2,3},{3,4},{4,5},{5,6},{6,7},{8,9},{9,10},{10,11},{11... | collective-permute-start | bytes 49160 | tf_op jit(solution)/shard_map/ppermute | solution.py:14
  11.6 5.9 %collective-permute-start.1 = (bf16[64,128]{1,0:T(8,128)(2,1)S(1)}, bf16[64,128]{1,0:T(8,128)(2,1)S(1)}, u32[]{:S(2)}, u32[]{:S(2)}) collective-permute-start(bf16[64,128]{1,0:T(8,128)(2,1)S(1)} %get-tuple-element.8), channel_id=1, source_target_pairs={{1,0},{2,1},{3,2},{4,3},{5,4},{6,5},{7,6},{9,8},{10,9},{11,10},{12... | collective-permute-start | bytes 49160 | tf_op jit(solution)/shard_map/ppermute | solution.py:15
  46.9 0.7 copy-start.1
  49.4 1.1 copy-start.2
  53.0 51.1 %copy-start.3 = (s32[512]{0:T(512)S(1)}, s32[512]{0:T(512)}, u32[]{:S(2)}) copy-start(s32[512]{0:T(512)} %param.9) | copy-start | bytes 6148
  100.5 123.1 %collective-permute-start.2 = (bf16[64,128]{1,0:T(8,128)(2,1)S(1)}, bf16[64,128]{1,0:T(8,128)(2,1)S(1)}, u32[]{:S(2)}, u32[]{:S(2)}) collective-permute-start(bf16[64,128]{1,0:T(8,128)(2,1)S(1)} %get-tuple-element.5), channel_id=1, source_target_pairs={{0,1},{1,2},{2,3},{3,4},{4,5},{5,6},{6,7},{8,9},{9,10},{10,11},{11... | collective-permute-start | bytes 49160 | tf_op jit(solution)/shard_map/ppermute | solution.py:23
  102.8 120.8 %collective-permute-start.3 = (bf16[64,128]{1,0:T(8,128)(2,1)S(1)}, bf16[64,128]{1,0:T(8,128)(2,1)S(1)}, u32[]{:S(2)}, u32[]{:S(2)}) collective-permute-start(bf16[64,128]{1,0:T(8,128)(2,1)S(1)} %get-tuple-element.6), channel_id=1, source_target_pairs={{1,0},{2,1},{3,2},{4,3},{5,4},{6,5},{7,6},{9,8},{10,9},{11,10},{12... | collective-permute-start | bytes 49160 | tf_op jit(solution)/shard_map/ppermute | solution.py:23
  380.3 14.0 %collective-permute-start.5 = (f32[56,256]{1,0:T(8,128)S(1)}, f32[56,256]{1,0:T(8,128)S(1)}, u32[]{:S(2)}, u32[]{:S(2)}) collective-permute-start(f32[56,256]{1,0:T(8,128)S(1)} %fusion), channel_id=1, source_target_pairs={{0,16},{8,24},{16,32},{24,40},{32,48},{40,56},{48,64},{56,72},{64,... | collective-permute-start | bytes 172040
  382.2 12.1 %collective-permute-start.4 = (f32[56,256]{1,0:T(8,128)S(1)}, f32[56,256]{1,0:T(8,128)S(1)}, u32[]{:S(2)}, u32[]{:S(2)}) collective-permute-start(f32[56,256]{1,0:T(8,128)S(1)} %fusion), channel_id=1, source_target_pairs={{0,8},{8,16},{16,24},{24,32},{32,40},{40,48},{48,56},{56,64},{64,7... | collective-permute-start | bytes 172040
  384.1 10.1 %collective-permute-start.6 = (f32[14,256]{1,0:T(8,128)S(1)}, f32[14,256]{1,0:T(8,128)S(1)}, u32[]{:S(2)}, u32[]{:S(2)}) collective-permute-start(f32[14,256]{1,0:T(8,128)S(1)} %slice.42), channel_id=1, source_target_pairs={{0,24},{8,32},{16,40},{24,48},{32,56},{40,64},{48,72},{56,80},{64,... | collective-permute-start | bytes 43016
Sparse Core Ops, SparseCore 0:
  49.6 101.9 all-reduce.3
where the time goes:
time: 404 us; the launch traced here: 403 us
  blocking collectives  269 us (67%)
  other arithmetic  55.2 us (14%)
  local copies, waits for them, and re-layouts  33.2 us (8%)
  between operations  18.1 us (4%)
  starting transfers between devices  14.1 us (3%)
  waiting for transfers between devices  7.61 us (2%)
  matrix products  6.48 us (2%)
    unnamed x1, blocking collectives  153 us
    psum x1, blocking collectives, shards(): total_sq = lax.psum(partial_sq, ('dp', 'space'))  116 us
    scatter-add x1, other arithmetic, shards(): jax.ops.segment_sum(grad_g.reshape(rows * offsets, chans), index.reshape(...  42.8 us
    gather x2, local copies, waits for them, and re-layouts, shards(): gathered = jnp.take(padded, index, axis=0).reshape(rows, offsets * chans)  18.5 us
  transfers between devices with their start and end apart: 8, of which 1 were waited for; matrix products, arithmetic and copies ran while one was open for 14% of the time, Pallas kernels for 0%

commit v1 on v0

v1 whole, which is shorter than its diff:
```python
import functools

import jax
import jax.numpy as jnp
from jax import lax
from jax.experimental import pallas as pl
from jax.experimental.pallas import tpu as pltpu
from jax.sharding import PartitionSpec as P

F32 = jnp.float32
BF16 = jnp.bfloat16
MESH = pl.DeviceIdType.MESH
ORDERS = (("xp", "xq", "yp", "yq"), ("xq", "xp", "yq", "yp"), ("yp", "yq", "xp", "xq"), ("yq", "yp", "xq", "xp"))
NT = (((1,), (1,)), ((), ()))


def dot(a, b):
    return jnp.dot(a, b, preferred_element_type=F32)


def dot_nt(a, b):
    return lax.dot_general(a, b, NT, preferred_element_type=F32)


def body(n_dp, n_space, comm, feats, teacher, weight, nbrs, counts,
         out_x, out_w, out_loss,
         win, nbr_v, teach_v, w_v, w_t, hot, g_t, gw, part, rc, s0, r1, s1, r2, s2, r3, s3, r4, s4,
         rz, ag, gsend, grecv, lsum, lrecv,
         lsem, halo_s, halo_r, core_s, core_r, step_s, step_r, z_s, z_r, ag_s, ag_r, gh_s, gh_r, loss_s, loss_r):
    sites, chans = feats.shape
    outs = teacher.shape[1]
    offsets = nbrs.shape[0]
    edge = sites // 4
    slots = sites + 2 * edge
    nz = n_dp // 4
    z4 = nz // 4
    rows = offsets * chans // n_dp

    dp, sp = lax.axis_index("dp"), lax.axis_index("space")
    core = dp % 2
    z = (dp // 2) % nz
    xh = dp // (2 * nz)
    xl, y = sp // 4, sp % 4
    bit = {"xp": (xl + xh) % 2, "xq": xh, "yp": (y % 2 + y // 2) % 2, "yq": y // 2}
    x = 2 * xh + xl
    xq = (x + 2 * xl + 3) % 4
    peer = {
        "xp": (dp, (1 - xl) * 4 + y),
        "xq": (dp + (xq // 2 - xh) * 2 * nz, (xq % 2) * 4 + y),
        "yp": (dp, xl * 4 + y + 1 - 2 * (y % 2)),
        "yq": (dp, xl * 4 + (y + 2 * (y % 2) + 3) % 4),
        "core": (dp + 1 - 2 * core, sp),
    }

    def z_peer(zz):
        return (xh * 2 * nz + zz * 2 + core, sp)

    def sp_peer(step):
        return (dp, (sp + step) % n_space)

    def piece_of(space):
        l, w = space // 4, space % 4
        return ((l + xh) % 2) * 4 + ((w % 2 + w // 2) % 2) * 2 + w // 2

    def remote(src, dst, send, recv, device):
        return pltpu.make_async_remote_copy(
            src_ref=src, dst_ref=dst, send_sem=send, recv_sem=recv, device_id=device, device_id_type=MESH)

    sent = []

    def start(copy):
        if comm:
            copy.start()
            sent.append(copy)

    def got(copy):
        if comm:
            copy.wait_recv()

    own_in = pltpu.make_async_copy(feats, win.at[pl.ds(edge, sites)], lsem.at[0])
    nbr_in = pltpu.make_async_copy(nbrs, nbr_v, lsem.at[1])
    w_in = pltpu.make_async_copy(weight, w_v, lsem.at[2])
    t_in = pltpu.make_async_copy(teacher, teach_v, lsem.at[3])
    nbr_in.start()
    own_in.start()
    w_in.start()
    t_in.start()
    if comm:
        barrier = pltpu.get_barrier_semaphore()
        partners = [sp_peer(i) for i in range(1, n_space)] + [peer["xq"], peer["core"]]
        for device in partners:
            pl.semaphore_signal(barrier, inc=1, device_id=device, device_id_type=MESH)

        @pl.loop(1, nz)
        def _(i):
            pl.semaphore_signal(barrier, inc=1, device_id=z_peer((z + i) % nz), device_id_type=MESH)

        pl.semaphore_wait(barrier, len(partners) + nz - 1)

    halo_up = remote(feats.at[pl.ds(sites - edge, edge)], win.at[pl.ds(0, edge)], halo_s.at[0], halo_r.at[0], sp_peer(1))
    halo_dn = remote(feats.at[pl.ds(0, edge)], win.at[pl.ds(edge + sites, edge)], halo_s.at[1], halo_r.at[1],
                     sp_peer(n_space - 1))
    start(halo_up)
    start(halo_dn)

    nbr_in.wait()
    nbr_t = nbr_v[...]
    slot = lax.broadcasted_iota(jnp.int32, (slots, sites), 0)
    for k in range(offsets):
        hot[k] = (slot == nbr_t[k:k + 1, :]).astype(F32).astype(BF16)

    eye = (lax.broadcasted_iota(jnp.int32, (outs, outs), 0) == lax.broadcasted_iota(jnp.int32, (outs, outs), 1))
    eye = eye.astype(F32).astype(BF16)
    w_in.wait()
    for k in range(offsets):
        w_t[:, k * chans:(k + 1) * chans] = dot_nt(eye, w_v[k * chans:(k + 1) * chans, :]).astype(BF16)
    t_in.wait()
    teach_t = dot_nt(eye, teach_v[...])

    count = counts[...]
    flat = lax.broadcasted_iota(jnp.int32, count.shape, 0) * count.shape[1] + lax.broadcasted_iota(
        jnp.int32, count.shape, 1)
    limit = jnp.sum(jnp.where(flat == dp * n_space + sp, count, 0))
    total_count = jnp.sum(count)

    own_in.wait()
    got(halo_up)
    got(halo_dn)
    win_t = dot_nt(eye[:chans, :chans], win[...]).astype(BF16)
    for k in range(offsets):
        g_t[k * chans:(k + 1) * chans, :] = dot(win_t, hot[k]).astype(BF16)
    z_t = dot(w_t[...], g_t[...])
    at = lax.broadcasted_iota(jnp.int32, (outs, sites), 1)
    diff = jnp.where((at < limit - edge) | (at >= sites - edge), z_t - teach_t, F32(0.0))
    dz_t = (diff / outs).astype(BF16)
    square = jnp.sum((diff * diff).reshape(outs // 8, 8, sites), axis=0)
    lsum[0] = square[:, :128] + square[:, 128:]

    chain = ["core", "xp", "xq", "yp", "yq"]
    hop = 1
    while hop < nz:
        chain.append(hop)
        hop *= 2

    def loss_copy(i):
        if i < 5:
            device = peer[chain[i]]
        else:
            device = z_peer(z + chain[i] - 2 * chain[i] * ((z // chain[i]) % 2))
        return remote(lsum.at[i], lrecv.at[i], loss_s.at[i], loss_r.at[i], device)

    loss_copies = [loss_copy(i) for i in range(len(chain))]

    def loss_step(i):
        if i >= len(chain):
            return
        got(loss_copies[i])
        lsum[i + 1] = lsum[i] + lrecv[i]
        if i + 1 < len(chain):
            start(loss_copies[i + 1])

    start(loss_copies[0])

    held = [s0, s1, s2, s3, s4]
    come = [rc, r1, r2, r3, r4]
    core_copies = [remote(part.at[1 - core, s], rc.at[s], core_s.at[s], core_r.at[s], peer["core"]) for s in range(4)]
    step_copies = []
    for i in range(4):
        half = 8 >> i
        step_copies.append([
            remote(held[i].at[s, pl.ds((1 - bit[ORDERS[s][i]]) * half, half)], come[i + 1].at[s],
                   step_s.at[i, s], step_r.at[i, s], peer[ORDERS[s][i]]) for s in range(4)])

    def after_core(s):
        got(core_copies[s])

        @pl.loop(0, 16)
        def _(i):
            s0[s, i] = (part[core, s, i].astype(F32) + rc[s, i].astype(F32)).astype(BF16)
        start(step_copies[0][s])

    def after_step(i, s):
        got(step_copies[i][s])
        half = 8 >> i
        mine = bit[ORDERS[s][i]] * half
        for q in range(half):
            held[i + 1][s, q] = (held[i][s, mine + q].astype(F32) + come[i + 1][s, q].astype(F32)).astype(BF16)
        if i < 3:
            start(step_copies[i + 1][s])
        elif comm:
            for j in range(z4):
                to = s * z4 + j
                back = (to - z + nz) % nz

                @pl.when(back != 0)
                def _():
                    remote(s4.at[s, 0, j], rz.at[back], z_s.at[back], z_r.at[back], z_peer(to)).start()

    block = 2 * z4 * rows
    gw[:, block:, :] = jnp.zeros((2, gw.shape[1] - block, outs), F32)
    for s in range(4):
        dims = ORDERS[s]
        for h in range(2):
            base = (h * 4 + s) * block
            gw[h, :block, :] = dot_nt(g_t[base:base + block, :], dz_t)
            for j in range(z4):
                for c in range(2):
                    frame = gw[h, (j * 2 + c) * rows:(j * 2 + c) * rows + 64, :].astype(BF16)
                    for p in range(8):
                        val = {"xp": p // 4, "xq": h, "yp": (p // 2) % 2, "yq": p % 2}
                        index = 0
                        for d in dims:
                            index = index * 2 + val[d]
                        q = p % 4
                        part[c, s, index, j] = frame[16 * q:16 * q + 16, 128 * (p // 4):128 * (p // 4) + 128]
        start(core_copies[s])
        if s > 0:
            after_core(s - 1)
            loss_step(s - 1)
    after_core(3)

    def spread_part(first, last, acc):
        for k in range(first, last):
            d_t = dot(w_v[k * chans:(k + 1) * chans, :], dz_t).astype(BF16)
            acc = acc + dot_nt(d_t, hot[k])
        return acc

    spread = spread_part(0, offsets, jnp.zeros((chans, slots), F32))
    own = jnp.transpose(spread)
    gsend[0] = own[:edge].astype(BF16)
    gsend[1] = own[edge + sites:].astype(BF16)
    gh_dn = remote(gsend.at[0], grecv.at[0], gh_s.at[0], gh_r.at[0], sp_peer(n_space - 1))
    gh_up = remote(gsend.at[1], grecv.at[1], gh_s.at[1], gh_r.at[1], sp_peer(1))
    start(gh_dn)
    start(gh_up)
    loss_step(3)

    for s in range(4):
        after_step(0, s)
    loss_step(4)
    for s in range(4):
        after_step(1, s)
    loss_step(5)

    got(gh_dn)
    got(gh_up)
    out_x[edge:sites - edge, :] = own[2 * edge:sites].astype(BF16)
    out_x[:edge, :] = (own[edge:2 * edge] + grecv[1].astype(F32)).astype(BF16)
    out_x[sites - edge:, :] = (own[sites:sites + edge] + grecv[0].astype(F32)).astype(BF16)

    for s in range(4):
        after_step(2, s)
    loss_step(6)
    for s in range(4):
        after_step(3, s)
    loss_step(7)
    loss_step(8)

    total = s4[z // z4, 0, z % z4].astype(F32)
    if comm:
        for t in range(1, nz):
            incoming = remote(rz.at[t], rz.at[t], z_s.at[t], z_r.at[t], z_peer(z))
            incoming.wait_recv()
            total = total + rz[t].astype(F32)
    mine = piece_of(sp)
    ag[mine] = total
    ag_copies = []
    for u in range(1, n_space):
        copy = remote(ag.at[mine], ag.at[mine], ag_s.at[u], ag_r.at[u], sp_peer(u))
        start(copy)
    loss_total = jnp.sum(lsum[len(chain)])
    out_loss[0, 0] = 0.5 * loss_total / (outs * total_count.astype(F32))
    if comm:
        for u in range(1, n_space):
            source = piece_of((sp - u + n_space) % n_space)
            remote(ag.at[source], ag.at[source], ag_s.at[u], ag_r.at[u], sp_peer(u)).wait_recv()
    for p in range(8):
        q, h = p % 4, p // 4
        keep = min(16, rows - 16 * q)
        out_w[16 * q:16 * q + keep, 128 * h:128 * h + 128] = ag[p][:keep]
    for copy in sent:
        copy.wait_send()
    if comm:
        for t in range(1, nz):
            remote(rz.at[t], rz.at[t], z_s.at[t], z_r.at[t], z_peer(z)).wait_send()


def shards(n_dp, n_space, comm, features, teacher, weight, neighbours, counts):
    sites, chans = features.shape
    outs = teacher.shape[1]
    offsets = neighbours.shape[1]
    edge = sites // 4
    slots = sites + 2 * edge
    nz = n_dp // 4
    z4 = nz // 4
    rows = offsets * chans // n_dp
    assert 48 < rows <= 64 and n_space == 8 and outs == 256 and chans == 128
    n_loss = 5 + (nz - 1).bit_length()
    tile = (16, 128)
    levels = []
    for i in range(1, 5):
        levels += [pltpu.VMEM((4, 16 >> i, z4) + tile, BF16)] * 2
    dma = pltpu.SemaphoreType.DMA
    grad_x, grad_w, loss = pl.pallas_call(
        functools.partial(body, n_dp, n_space, comm),
        out_shape=(
            jax.ShapeDtypeStruct((sites, chans), BF16),
            jax.ShapeDtypeStruct((rows, outs), F32),
            jax.ShapeDtypeStruct((1, 1), F32),
        ),
        in_specs=[pl.BlockSpec(memory_space=pl.ANY)] * 4 + [pl.BlockSpec(memory_space=pltpu.VMEM)],
        out_specs=(
            pl.BlockSpec(memory_space=pltpu.VMEM),
            pl.BlockSpec(memory_space=pltpu.VMEM),
            pl.BlockSpec(memory_space=pltpu.SMEM),
        ),
        scratch_shapes=[
            pltpu.VMEM((slots, chans), BF16),
            pltpu.VMEM((offsets, sites), jnp.int32),
            pltpu.VMEM((sites, outs), BF16),
            pltpu.VMEM((offsets * chans, outs), BF16),
            pltpu.VMEM((outs, offsets * chans), BF16),
            pltpu.VMEM((offsets, slots, sites), BF16),
            pltpu.VMEM((offsets * chans, sites), BF16),
            pltpu.VMEM((2, 2 * z4 * rows + 16, outs), F32),
            pltpu.VMEM((2, 4, 16, z4) + tile, BF16),
            pltpu.VMEM((4, 16, z4) + tile, BF16),
            pltpu.VMEM((4, 16, z4) + tile, BF16),
        ] + levels + [
            pltpu.VMEM((nz,) + tile, BF16),
            pltpu.VMEM((8,) + tile, F32),
            pltpu.VMEM((2, edge, chans), BF16),
            pltpu.VMEM((2, edge, chans), BF16),
            pltpu.VMEM((n_loss + 1, 8, 128), F32),
            pltpu.VMEM((n_loss, 8, 128), F32),
            dma((4,)), dma((2,)), dma((2,)), dma((4,)), dma((4,)), dma((4, 4)), dma((4, 4)),
            dma((nz,)), dma((nz,)), dma((n_space,)), dma((n_space,)), dma((2,)), dma((2,)),
            dma((n_loss,)), dma((n_loss,)),
        ],
        compiler_params=pltpu.CompilerParams(
            vmem_limit_bytes=48 * 1024 * 1024,
            **(dict(collective_id=0, has_side_effects=True) if comm else {})),
    )(features, teacher, weight, neighbours.T, counts.reshape(-1, 128))
    return grad_x, grad_w, loss.reshape(())


def solution(mesh, comm=True):
    placed = (
        P(("dp", "space"), None),
        P(("dp", "space"), None),
        P(),
        P(("dp", "space"), None),
        P(),
    )
    return jax.shard_map(
        functools.partial(shards, mesh.shape["dp"], mesh.shape["space"], comm),
        mesh=mesh,
        in_specs=placed,
        out_specs=(P(("dp", "space"), None), P("dp", None), P()),
        check_vma=False,
    )
```

time: 404 us -> 70.9 us (0.18)
  the two profiles are of different devices: /device:TPU:4 before, /device:TPU:2 now
where the time goes in v1:
time: 70.9 us; the launch traced here: 70.6 us
  Pallas kernels  62.3 us (88%)
  local copies, waits for them, and re-layouts  5.9 us (8%)
  between operations  2.34 us (3%)
    pallas_call x1, Pallas kernels, shards(): pl.pallas_call(functools.partial(body, n_dp, n_space, comm), out_shape=(j...  62.3 us
    unnamed x12, local copies, waits for them, and re-layouts  5.9 us

profile of v1, /device:TPU:2, one launch (start us, length us, event | category | flops | bytes accessed | tf_op | source)
XLA Modules:
  0.0 70.6 jit_solution(5858291255749053046)
XLA Ops:
  0.6 0.0 copy-start
  0.6 1.5 %copy-done = bf16[3456,256]{1,0:T(8,128)(2,1)S(1)} copy-done((bf16[3456,256]{1,0:T(8,128)(2,1)S(1)}, bf16[3456,256]{1,0:T(8,128)(2,1)}, u32[]{:S(2)}) %copy-start) | copy-done | bytes 1769496
  2.1 0.0 copy-start.1
  2.1 0.9 %copy-done.1 = bf16[256,256]{1,0:T(8,128)(2,1)S(1)} copy-done((bf16[256,256]{1,0:T(8,128)(2,1)S(1)}, bf16[256,256]{1,0:T(8,128)(2,1)}, u32[]{:S(2)}) %copy-start.1) | copy-done | bytes 131096
  3.0 0.0 copy-start.2
  3.0 0.8 %copy-done.2 = bf16[256,128]{1,0:T(8,128)(2,1)S(1)} copy-done((bf16[256,128]{1,0:T(8,128)(2,1)S(1)}, bf16[256,128]{1,0:T(8,128)(2,1)}, u32[]{:S(2)}) %copy-start.2) | copy-done | bytes 65560
  3.9 0.0 copy-start.3
  3.9 0.8 %copy-done.3 = s32[256,27]{0,1:T(8,128)S(1)} copy-done((s32[256,27]{0,1:T(8,128)S(1)}, s32[256,27]{0,1:T(8,128)}, u32[]{:S(2)}) %copy-start.3) | copy-done | bytes 27672
  4.6 0.0 copy-start.4
  4.6 0.7 copy-done.4
  5.3 62.3 %shard_map.76 = (bf16[256,128]{1,0:T(8,128)(2,1)S(1)}, f32[54,256]{1,0:T(8,128)S(1)}, f32[1,1]{1,0:T(1,128)}) custom-call(bf16[256,128]{1,0:T(8,128)(2,1)S(1)} %copy-done.2, bf16[256,256]{1,0:T(8,128)(2,1)S(1)} %copy-done.1, bf16[3456,256]{1,0:T(8,128)(2,1)S(1)} %copy-done, s32[27,256]{1,0:T(8,128)S(1)} %bitcast.3, s32[4,128]{1,0:T(4,128)S(1)} %bitcast.4), custom_call_target="tpu_custom_call" | custom-call | tf_op jit(solution)/shard_map/pallas_call | solution.py:304
  67.6 0.6 copy.11
  68.3 0.6 copy.12
Async XLA Ops:
  0.6 1.5 %copy-start = (bf16[3456,256]{1,0:T(8,128)(2,1)S(1)}, bf16[3456,256]{1,0:T(8,128)(2,1)}, u32[]{:S(2)}) copy-start(bf16[3456,256]{1,0:T(8,128)(2,1)} %weight.1) | copy-start | bytes 5308420
  2.1 0.9 %copy-start.1 = (bf16[256,256]{1,0:T(8,128)(2,1)S(1)}, bf16[256,256]{1,0:T(8,128)(2,1)}, u32[]{:S(2)}) copy-start(bf16[256,256]{1,0:T(8,128)(2,1)} %teacher.1) | copy-start | bytes 393220
  3.0 0.8 %copy-start.2 = (bf16[256,128]{1,0:T(8,128)(2,1)S(1)}, bf16[256,128]{1,0:T(8,128)(2,1)}, u32[]{:S(2)}) copy-start(bf16[256,128]{1,0:T(8,128)(2,1)} %feats.1) | copy-start | bytes 196612
  3.9 0.8 %copy-start.3 = (s32[256,27]{0,1:T(8,128)S(1)}, s32[256,27]{0,1:T(8,128)}, u32[]{:S(2)}) copy-start(s32[256,27]{0,1:T(8,128)} %param.8) | copy-start | bytes 82948
  4.6 0.7 copy-start.4

commit v2 on v1

v2 whole, which is shorter than its diff:
```python
import functools

import jax
import jax.numpy as jnp
from jax import lax
from jax.experimental import pallas as pl
from jax.experimental.pallas import tpu as pltpu
from jax.sharding import PartitionSpec as P

F32 = jnp.float32
BF16 = jnp.bfloat16
MESH = pl.DeviceIdType.MESH
NT = (((1,), (1,)), ((), ()))


def dot(a, b):
    return jnp.dot(a, b, preferred_element_type=F32)


def dot_nt(a, b):
    return lax.dot_general(a, b, NT, preferred_element_type=F32)


def body(n_dp, n_space, comm, feats, teacher, weight, nbrs, counts,
         to_x, to_w, out_loss,
         out_x, out_w,
         win, nbr_v, count_v, teach_v, w_v, w_t, hot, g_t, gw, part, rc, s0, r1, s1, r2, s2,
         rz, ag, gsend, grecv, lsum, lrecv,
         greeted, lsem, halo_s, halo_r, core_s, core_r, ring_s, ring_r, z_s, z_r, ag_s, ag_r, gh_s, gh_r, loss_s, loss_r):
    sites, chans = feats.shape
    outs = teacher.shape[1]
    offsets = nbrs.shape[0]
    edge = sites // 4
    slots = sites + 2 * edge
    nz = n_dp // 4
    z4 = nz // 4
    rows = offsets * chans // n_dp

    dp, sp = lax.axis_index("dp"), lax.axis_index("space")
    core = dp % 2
    z = (dp // 2) % nz
    xh = dp // (2 * nz)
    xl, y = sp // 4, sp % 4
    x = 2 * xh + xl

    def x_peer(step):
        to = (x + step) % 4
        return (dp + (to // 2 - xh) * 2 * nz, (to % 2) * 4 + y)

    def y_peer(step):
        return (dp, xl * 4 + (y + step) % 4)

    core_peer = (dp + 1 - 2 * core, sp)

    def z_peer(zz):
        return (xh * 2 * nz + zz * 2 + core, sp)

    def sp_peer(step):
        return (dp, (sp + step) % n_space)

    def remote(src, dst, send, recv, device):
        return pltpu.make_async_remote_copy(
            src_ref=src, dst_ref=dst, send_sem=send, recv_sem=recv, device_id=device, device_id_type=MESH)

    sent = []

    def start(copy):
        if comm:
            copy.start()
            sent.append(copy)

    def got(copy):
        if comm:
            copy.wait_recv()

    own_in = pltpu.make_async_copy(feats, win.at[pl.ds(edge, sites)], lsem.at[0])
    nbr_in = pltpu.make_async_copy(nbrs, nbr_v, lsem.at[1])
    w_in = pltpu.make_async_copy(weight, w_v, lsem.at[2])
    t_in = pltpu.make_async_copy(teacher, teach_v, lsem.at[3])
    nbr_in.start()
    own_in.start()
    w_in.start()
    t_in.start()
    c_in = pltpu.make_async_copy(counts, count_v, lsem.at[4])
    c_in.start()
    if comm:
        barrier = pltpu.get_barrier_semaphore()
        partners = [sp_peer(1), sp_peer(n_space - 1), z_peer((z + 1) % nz), z_peer((z + nz - 1) % nz)]
        partners += [x_peer(i) for i in (1, 3, 2)] + [y_peer(i) for i in (1, 3, 2)] + [core_peer]
        for device in partners:
            pl.semaphore_signal(barrier, inc=1, device_id=device, device_id_type=MESH)
        pl.semaphore_wait(barrier, len(partners))

    def greet(i):
        if comm and 2 ** i < nz // 2:
            for step in (2 ** i, nz - 2 ** i):
                pl.semaphore_signal(greeted.at[i], inc=1, device_id=z_peer((z + step) % nz), device_id_type=MESH)

    def greetings(i):
        if comm and 2 ** i < nz // 2:
            pl.semaphore_wait(greeted.at[i], 2)
            greet(i + 1)

    halo_up = remote(feats.at[pl.ds(sites - edge, edge)], win.at[pl.ds(0, edge)], halo_s.at[0], halo_r.at[0], sp_peer(1))
    halo_dn = remote(feats.at[pl.ds(0, edge)], win.at[pl.ds(edge + sites, edge)], halo_s.at[1], halo_r.at[1],
                     sp_peer(n_space - 1))
    start(halo_up)
    start(halo_dn)
    greet(0)

    nbr_in.wait()
    nbr_t = nbr_v[...]
    slot = lax.broadcasted_iota(jnp.int32, (slots, sites), 0)
    for k in range(offsets):
        hot[k] = (slot == nbr_t[k:k + 1, :]).astype(F32).astype(BF16)

    eye = (lax.broadcasted_iota(jnp.int32, (outs, outs), 0) == lax.broadcasted_iota(jnp.int32, (outs, outs), 1))
    eye = eye.astype(F32).astype(BF16)
    w_in.wait()
    for k in range(offsets):
        w_t[:, k * chans:(k + 1) * chans] = dot_nt(eye, w_v[k * chans:(k + 1) * chans, :]).astype(BF16)
    t_in.wait()
    teach_t = dot_nt(eye, teach_v[...])

    c_in.wait()
    count = count_v[...]
    flat = lax.broadcasted_iota(jnp.int32, count.shape, 0) * count.shape[1] + lax.broadcasted_iota(
        jnp.int32, count.shape, 1)
    limit = jnp.sum(jnp.where(flat == dp * n_space + sp, count, 0))
    total_count = jnp.sum(count)

    own_in.wait()
    got(halo_up)
    got(halo_dn)
    win_t = dot_nt(eye[:chans, :chans], win[...]).astype(BF16)
    for k in range(offsets):
        g_t[k * chans:(k + 1) * chans, :] = dot(win_t, hot[k]).astype(BF16)
    greetings(0)
    z_t = dot(w_t[...], g_t[...])
    at = lax.broadcasted_iota(jnp.int32, (outs, sites), 1)
    diff = jnp.where((at < limit - edge) | (at >= sites - edge), z_t - teach_t, F32(0.0))
    dz_t = (diff / outs).astype(BF16)
    square = jnp.sum((diff * diff).reshape(outs // 8, 8, sites), axis=0)
    lsum[0] = square[:, :128] + square[:, 128:]

    chain = [core_peer, x_peer(1 - 2 * (x % 2)), x_peer(2), y_peer(1 - 2 * (y % 2)), y_peer(2)]
    hop = 1
    while hop < nz:
        chain.append(z_peer(z + hop - 2 * hop * ((z // hop) % 2)))
        hop *= 2
    loss_copies = [remote(lsum.at[i], lrecv.at[i], loss_s.at[i], loss_r.at[i], chain[i]) for i in range(len(chain))]

    def loss_step(i):
        got(loss_copies[i])
        lsum[i + 1] = lsum[i] + lrecv[i]
        if i + 1 < len(chain):
            start(loss_copies[i + 1])

    start(loss_copies[0])

    core_copies = [remote(part.at[1 - core, s], rc.at[s], core_s.at[s], core_r.at[s], core_peer) for s in range(4)]

    def ring(s, level):
        return (x, x_peer) if (s < 2) == (level == 0) else (y, y_peer)

    steps = (1, 3, 2)
    ring_copies = [[[remote((s0, s1)[level].at[s, (ring(s, level)[0] + t) % 4], (r1, r2)[level].at[s, t],
                            ring_s.at[level, s, t], ring_r.at[level, s, t], ring(s, level)[1](t))
                     for t in steps] for s in range(4)] for level in range(2)]

    def after_core(s):
        got(core_copies[s])

        @pl.loop(0, 4)
        def _(i):
            s0[s, i] = (part[core, s, i].astype(F32) + rc[s, i].astype(F32)).astype(BF16)
        for copy in ring_copies[0][s]:
            start(copy)

    def after_x(s):
        for copy in ring_copies[0][s]:
            got(copy)
        mine = ring(s, 0)[0]
        for i in range(4):
            add = [s0[s, mine, i]] + [r1[s, t, i] for t in steps]
            s1[s, i] = sum(v.astype(F32) for v in add).astype(BF16)
        for copy in ring_copies[1][s]:
            start(copy)

    def after_y(s):
        for copy in ring_copies[1][s]:
            got(copy)
        add = [s1[s, ring(s, 1)[0]]] + [r2[s, t] for t in steps]
        s2[s] = sum(v.astype(F32) for v in add).astype(BF16)
        if comm:
            for j in range(z4):
                to = s * z4 + j
                back = (to - z + nz) % nz

                @pl.when(back != 0)
                def _():
                    remote(s2.at[s, j], rz.at[back], z_s.at[back], z_r.at[back], z_peer(to)).start()

    block = 2 * z4 * rows
    gw[:, block:, :] = jnp.zeros((2, gw.shape[1] - block, outs), F32)
    before = None
    for s in (0, 2, 1, 3):
        for h in range(2):
            base = (h * 4 + s) * block
            gw[h, :block, :] = dot_nt(g_t[base:base + block, :], dz_t)
            for j in range(z4):
                for c in range(2):
                    frame = gw[h, (j * 2 + c) * rows:(j * 2 + c) * rows + 64, :].astype(BF16)
                    for l in range(2):
                        for q in range(4):
                            at = (2 * h + l, q) if s < 2 else (q, 2 * h + l)
                            part[c, s, at[0], at[1], j] = frame[16 * q:16 * q + 16, 128 * l:128 * l + 128]
        start(core_copies[s])
        if before is not None:
            after_core(before)
        before = s
        if s == 1:
            loss_step(0)
            greetings(1)
    after_core(before)
    loss_step(1)
    greetings(2)

    def spread_part(first, last, acc):
        for k in range(first, last):
            d_t = dot(w_v[k * chans:(k + 1) * chans, :], dz_t).astype(BF16)
            acc = acc + dot_nt(d_t, hot[k])
        return acc

    spread = spread_part(0, offsets, jnp.zeros((chans, slots), F32))
    own = jnp.transpose(spread)
    gsend[0] = own[:edge].astype(BF16)
    gsend[1] = own[edge + sites:].astype(BF16)
    gh_dn = remote(gsend.at[0], grecv.at[0], gh_s.at[0], gh_r.at[0], sp_peer(n_space - 1))
    gh_up = remote(gsend.at[1], grecv.at[1], gh_s.at[1], gh_r.at[1], sp_peer(1))
    start(gh_dn)
    start(gh_up)
    loss_step(2)

    for s in (0, 2, 1, 3):
        after_x(s)
    loss_step(3)

    got(gh_dn)
    got(gh_up)
    out_x[edge:sites - edge, :] = own[2 * edge:sites].astype(BF16)
    out_x[:edge, :] = (own[edge:2 * edge] + grecv[1].astype(F32)).astype(BF16)
    out_x[sites - edge:, :] = (own[sites:sites + edge] + grecv[0].astype(F32)).astype(BF16)

    x_out = pltpu.make_async_copy(out_x, to_x, lsem.at[5])
    x_out.start()

    loss_step(4)
    for s in (0, 2, 1, 3):
        after_y(s)
    loss_step(5)
    loss_step(6)
    loss_step(7)

    total = s2[z // z4, z % z4].astype(F32)
    if comm:
        for t in range(1, nz):
            incoming = remote(rz.at[t], rz.at[t], z_s.at[t], z_r.at[t], z_peer(z))
            incoming.wait_recv()
            total = total + rz[t].astype(F32)
    ag[sp] = total
    ag_copies = []
    for u in range(1, n_space):
        copy = remote(ag.at[sp], ag.at[sp], ag_s.at[u], ag_r.at[u], sp_peer(u))
        start(copy)
    loss_step(8)
    loss_total = jnp.sum(lsum[len(chain)])
    out_loss[0, 0] = 0.5 * loss_total / (outs * total_count.astype(F32))
    if comm:
        for u in range(1, n_space):
            source = (sp - u + n_space) % n_space
            remote(ag.at[source], ag.at[source], ag_s.at[u], ag_r.at[u], sp_peer(u)).wait_recv()
    for p in range(8):
        q, h = p % 4, p // 4
        keep = min(16, rows - 16 * q)
        out_w[16 * q:16 * q + keep, 128 * h:128 * h + 128] = ag[p][:keep]
    w_out = pltpu.make_async_copy(out_w, to_w, lsem.at[6])
    w_out.start()
    for copy in sent:
        copy.wait_send()
    if comm:
        for t in range(1, nz):
            remote(rz.at[t], rz.at[t], z_s.at[t], z_r.at[t], z_peer(z)).wait_send()
    x_out.wait()
    w_out.wait()


def finish(x_in, w_in, x_out, w_out, x_v, w_v, sem):
    first = [pltpu.make_async_copy(x_in, x_v, sem.at[0]), pltpu.make_async_copy(w_in, w_v, sem.at[1])]
    second = [pltpu.make_async_copy(x_v, x_out, sem.at[2]), pltpu.make_async_copy(w_v, w_out, sem.at[3])]
    for copy in first:
        copy.start()
    for copy, then in zip(first, second):
        copy.wait()
        then.start()
    for copy in second:
        copy.wait()


def shards(n_dp, n_space, comm, features, teacher, weight, neighbours, counts):
    sites, chans = features.shape
    outs = teacher.shape[1]
    offsets = neighbours.shape[1]
    edge = sites // 4
    slots = sites + 2 * edge
    nz = n_dp // 4
    z4 = nz // 4
    rows = offsets * chans // n_dp
    assert 48 < rows <= 64 and n_space == 8 and outs == 256 and chans == 128
    n_loss = 5 + (nz - 1).bit_length()
    tile = (16, 128)
    dma = pltpu.SemaphoreType.DMA
    results = (
        jax.ShapeDtypeStruct((sites, chans), BF16),
        jax.ShapeDtypeStruct((rows, outs), F32),
        jax.ShapeDtypeStruct((1, 1), F32),
    )
    done = pl.pallas_call(
        functools.partial(body, n_dp, n_space, comm),
        out_shape=results,
        in_specs=[pl.BlockSpec(memory_space=pl.ANY)] * 5,
        out_specs=(
            pl.BlockSpec(memory_space=pl.ANY),
            pl.BlockSpec(memory_space=pl.ANY),
            pl.BlockSpec(memory_space=pltpu.SMEM),
        ),
        scratch_shapes=[
            pltpu.VMEM((sites, chans), BF16),
            pltpu.VMEM((rows, outs), F32),
            pltpu.VMEM((slots, chans), BF16),
            pltpu.VMEM((offsets, sites), jnp.int32),
            pltpu.VMEM((n_dp * n_space // 128, 128), jnp.int32),
            pltpu.VMEM((sites, outs), BF16),
            pltpu.VMEM((offsets * chans, outs), BF16),
            pltpu.VMEM((outs, offsets * chans), BF16),
            pltpu.VMEM((offsets, slots, sites), BF16),
            pltpu.VMEM((offsets * chans, sites), BF16),
            pltpu.VMEM((2, 2 * z4 * rows + 16, outs), F32),
            pltpu.VMEM((2, 4, 4, 4, z4) + tile, BF16),
            pltpu.VMEM((4, 4, 4, z4) + tile, BF16),
            pltpu.VMEM((4, 4, 4, z4) + tile, BF16),
            pltpu.VMEM((4, 4, 4, z4) + tile, BF16),
            pltpu.VMEM((4, 4, z4) + tile, BF16),
            pltpu.VMEM((4, 4, z4) + tile, BF16),
            pltpu.VMEM((4, z4) + tile, BF16),
            pltpu.VMEM((nz,) + tile, BF16),
            pltpu.VMEM((8,) + tile, F32),
            pltpu.VMEM((2, edge, chans), BF16),
            pltpu.VMEM((2, edge, chans), BF16),
            pltpu.VMEM((n_loss + 1, 8, 128), F32),
            pltpu.VMEM((n_loss, 8, 128), F32),
            pltpu.SemaphoreType.REGULAR((3,)),
            dma((7,)), dma((2,)), dma((2,)), dma((4,)), dma((4,)), dma((2, 4, 4)), dma((2, 4, 4)),
            dma((nz,)), dma((nz,)), dma((n_space,)), dma((n_space,)), dma((2,)), dma((2,)),
            dma((n_loss,)), dma((n_loss,)),
        ],
        compiler_params=pltpu.CompilerParams(
            vmem_limit_bytes=56 * 1024 * 1024,
            **(dict(collective_id=0, has_side_effects=True) if comm else {})),
    )(features, teacher, weight, neighbours.T, counts.reshape(-1, 128))
    anywhere = [pl.BlockSpec(memory_space=pl.ANY)] * 2
    grad_x, grad_w = pl.pallas_call(
        finish, out_shape=results[:2], in_specs=anywhere, out_specs=tuple(anywhere),
        scratch_shapes=[pltpu.VMEM((sites, chans), BF16), pltpu.VMEM((rows, outs), F32), dma((4,))],
        compiler_params=pltpu.CompilerParams(vmem_limit_bytes=56 * 1024 * 1024),
    )(*done[:2])
    return grad_x, grad_w, done[2].reshape(())


def solution(mesh, comm=True):
    placed = (
        P(("dp", "space"), None),
        P(("dp", "space"), None),
        P(),
        P(("dp", "space"), None),
        P(),
    )
    return jax.shard_map(
        functools.partial(shards, mesh.shape["dp"], mesh.shape["space"], comm),
        mesh=mesh,
        in_specs=placed,
        out_specs=(P(("dp", "space"), None), P("dp", None), P()),
        check_vma=False,
    )
```

time: 70.9 us -> 60.1 us (0.85)
  the two profiles are of different devices: /device:TPU:2 before, /device:TPU:4 now
where the time goes in v2:
time: 60.1 us; the launch traced here: 59.9 us
  Pallas kernels  57.6 us (96%)
  between operations  2.4 us (4%)
    pallas_call x1, Pallas kernels, shards(): pl.pallas_call(functools.partial(body, n_dp, n_space, comm), out_shape=re...  56 us
    pallas_call x1, Pallas kernels, shards(): pl.pallas_call(finish, out_shape=results[:2], in_specs=anywhere, out_spec...  1.52 us

profile of v2, /device:TPU:4, one launch (start us, length us, event | category | flops | bytes accessed | tf_op | source)
XLA Modules:
  0.0 59.9 jit_solution(5444611294423017473)
XLA Ops:
  0.6 56.0 %shard_map.76 = (bf16[256,128]{1,0:T(8,128)(2,1)}, f32[54,256]{1,0:T(8,128)}, f32[1,1]{1,0:T(1,128)}) custom-call(bf16[256,128]{1,0:T(8,128)(2,1)} %feats.1, bf16[256,256]{1,0:T(8,128)(2,1)} %teacher.1, bf16[3456,256]{1,0:T(8,128)(2,1)} %weight.1, s32[27,256]{1,0:T(8,128)} %bitcast.3, s32[4,128]{1,0:T(4,128)} %bitcast.4), custom_call_target="tpu_custom_call" | custom-call | tf_op jit(solution)/shard_map/pallas_call | solution.py:328
  56.7 1.5 %shard_map.77 = (bf16[256,128]{1,0:T(8,128)(2,1)}, f32[54,256]{1,0:T(8,128)}) custom-call(bf16[256,128]{1,0:T(8,128)(2,1)} %get-tuple-element.8.x_in, f32[54,256]{1,0:T(8,128)} %get-tuple-element.9.w_in), custom_call_target="tpu_custom_call" | custom-call | tf_op jit(solution)/shard_map/pallas_call | solution.py:372

commit v3 on v2

--- a/solution.py
+++ b/solution.py
@@ -73,22 +73,24 @@
         if comm:
             copy.wait_recv()
 
-    own_in = pltpu.make_async_copy(feats, win.at[pl.ds(edge, sites)], lsem.at[0])
+    own_in = pltpu.make_async_copy(feats, win.at[pl.ds(0, sites)], lsem.at[0])
     nbr_in = pltpu.make_async_copy(nbrs, nbr_v, lsem.at[1])
     w_in = pltpu.make_async_copy(weight, w_v, lsem.at[2])
     t_in = pltpu.make_async_copy(teacher, teach_v, lsem.at[3])
-    nbr_in.start()
-    own_in.start()
-    w_in.start()
-    t_in.start()
-    c_in = pltpu.make_async_copy(counts, count_v, lsem.at[4])
-    c_in.start()
     if comm:
         barrier = pltpu.get_barrier_semaphore()
         partners = [sp_peer(1), sp_peer(n_space - 1), z_peer((z + 1) % nz), z_peer((z + nz - 1) % nz)]
         partners += [x_peer(i) for i in (1, 3, 2)] + [y_peer(i) for i in (1, 3, 2)] + [core_peer]
         for device in partners:
             pl.semaphore_signal(barrier, inc=1, device_id=device, device_id_type=MESH)
+    own_in.start()
+    nbr_in.start()
+    w_in.start()
+    t_in.start()
+    c_in = pltpu.make_async_copy(counts, count_v, lsem.at[4])
+    c_in.start()
+    own_in.wait()
+    if comm:
         pl.semaphore_wait(barrier, len(partners))
 
     def greet(i):
@@ -101,8 +103,8 @@
             pl.semaphore_wait(greeted.at[i], 2)
             greet(i + 1)
 
-    halo_up = remote(feats.at[pl.ds(sites - edge, edge)], win.at[pl.ds(0, edge)], halo_s.at[0], halo_r.at[0], sp_peer(1))
-    halo_dn = remote(feats.at[pl.ds(0, edge)], win.at[pl.ds(edge + sites, edge)], halo_s.at[1], halo_r.at[1],
+    halo_up = remote(win.at[pl.ds(sites - edge, edge)], win.at[pl.ds(sites, edge)], halo_s.at[0], halo_r.at[0], sp_peer(1))
+    halo_dn = remote(win.at[pl.ds(0, edge)], win.at[pl.ds(sites + edge, edge)], halo_s.at[1], halo_r.at[1],
                      sp_peer(n_space - 1))
     start(halo_up)
     start(halo_dn)
@@ -110,6 +112,8 @@
 
     nbr_in.wait()
     nbr_t = nbr_v[...]
+    nbr_t = jnp.where((nbr_t >= edge) & (nbr_t < edge + sites), nbr_t - edge,
+                      jnp.where((nbr_t >= 0) & (nbr_t < edge), nbr_t + sites, nbr_t))
     slot = lax.broadcasted_iota(jnp.int32, (slots, sites), 0)
     for k in range(offsets):
         hot[k] = (slot == nbr_t[k:k + 1, :]).astype(F32).astype(BF16)
@@ -129,12 +133,15 @@
     limit = jnp.sum(jnp.where(flat == dp * n_space + sp, count, 0))
     total_count = jnp.sum(count)
 
-    own_in.wait()
+    own_t = dot_nt(eye[:chans, :chans], win[:sites, :]).astype(BF16)
+    for k in range(offsets):
+        g_t[k * chans:(k + 1) * chans, :] = dot(own_t, hot[k, :sites, :]).astype(BF16)
     got(halo_up)
     got(halo_dn)
-    win_t = dot_nt(eye[:chans, :chans], win[...]).astype(BF16)
+    edge_t = dot_nt(eye[:chans, :chans], win[sites:, :]).astype(BF16)
     for k in range(offsets):
-        g_t[k * chans:(k + 1) * chans, :] = dot(win_t, hot[k]).astype(BF16)
+        at = slice(k * chans, (k + 1) * chans)
+        g_t[at, :] = (g_t[at, :].astype(F32) + dot(edge_t, hot[k, sites:, :])).astype(BF16)
     greetings(0)
     z_t = dot(w_t[...], g_t[...])
     at = lax.broadcasted_iota(jnp.int32, (outs, sites), 1)
@@ -143,20 +150,30 @@
     square = jnp.sum((diff * diff).reshape(outs // 8, 8, sites), axis=0)
     lsum[0] = square[:, :128] + square[:, 128:]
 
-    chain = [core_peer, x_peer(1 - 2 * (x % 2)), x_peer(2), y_peer(1 - 2 * (y % 2)), y_peer(2)]
-    hop = 1
-    while hop < nz:
-        chain.append(z_peer(z + hop - 2 * hop * ((z // hop) % 2)))
-        hop *= 2
-    loss_copies = [remote(lsum.at[i], lrecv.at[i], loss_s.at[i], loss_r.at[i], chain[i]) for i in range(len(chain))]
-
-    def loss_step(i):
-        got(loss_copies[i])
-        lsum[i + 1] = lsum[i] + lrecv[i]
-        if i + 1 < len(chain):
-            start(loss_copies[i + 1])
-
-    start(loss_copies[0])
+    def loss_stage(stage, place, size, device, base):
+        come = lrecv.at[pl.ds(base, size)]
+
+        def copy(t, source):
+            return remote(lsum.at[stage], come.at[source], loss_s.at[base + t], loss_r.at[base + t], device(t))
+
+        def send():
+            come[place] = lsum[stage]
+            for t in range(1, size):
+                start(copy(t, place))
+
+        def collect():
+            for t in range(1, size):
+                got(copy(t, (place - t + size) % size))
+            lsum[stage + 1] = sum(come[i] for i in range(1, size)) + come[0]
+
+        return send, collect
+
+    stages = [
+        loss_stage(0, z, nz, lambda t: z_peer((z + t) % nz), 0),
+        loss_stage(1, x, 4, x_peer, nz),
+        loss_stage(2, y, 4, y_peer, nz + 4),
+        loss_stage(3, core, 2, lambda t: core_peer, nz + 8),
+    ]
 
     core_copies = [remote(part.at[1 - core, s], rc.at[s], core_s.at[s], core_r.at[s], core_peer) for s in range(4)]
 
@@ -187,10 +204,13 @@
         for copy in ring_copies[1][s]:
             start(copy)
 
-    def after_y(s):
-        for copy in ring_copies[1][s]:
-            got(copy)
-        add = [s1[s, ring(s, 1)[0]]] + [r2[s, t] for t in steps]
+    def after_y(ahead):
+        s = (z // z4 + ahead) % 4
+        for t in steps:
+            if comm:
+                remote(r2.at[s, t], r2.at[s, t], ring_s.at[1, s, t], ring_r.at[1, s, t], core_peer).wait_recv()
+        first = s // 2
+        add = [s1[s, y + first * (x - y)]] + [r2[s, t] for t in steps]
         s2[s] = sum(v.astype(F32) for v in add).astype(BF16)
         if comm:
             for j in range(z4):
@@ -220,11 +240,10 @@
             after_core(before)
         before = s
         if s == 1:
-            loss_step(0)
             greetings(1)
     after_core(before)
-    loss_step(1)
     greetings(2)
+    stages[0][0]()
 
     def spread_part(first, last, acc):
         for k in range(first, last):
@@ -234,33 +253,30 @@
 
     spread = spread_part(0, offsets, jnp.zeros((chans, slots), F32))
     own = jnp.transpose(spread)
-    gsend[0] = own[:edge].astype(BF16)
-    gsend[1] = own[edge + sites:].astype(BF16)
+    gsend[0] = own[sites:sites + edge].astype(BF16)
+    gsend[1] = own[sites + edge:].astype(BF16)
     gh_dn = remote(gsend.at[0], grecv.at[0], gh_s.at[0], gh_r.at[0], sp_peer(n_space - 1))
     gh_up = remote(gsend.at[1], grecv.at[1], gh_s.at[1], gh_r.at[1], sp_peer(1))
     start(gh_dn)
     start(gh_up)
-    loss_step(2)
 
     for s in (0, 2, 1, 3):
         after_x(s)
-    loss_step(3)
+    stages[0][1]()
+    stages[1][0]()
 
     got(gh_dn)
     got(gh_up)
-    out_x[edge:sites - edge, :] = own[2 * edge:sites].astype(BF16)
-    out_x[:edge, :] = (own[edge:2 * edge] + grecv[1].astype(F32)).astype(BF16)
-    out_x[sites - edge:, :] = (own[sites:sites + edge] + grecv[0].astype(F32)).astype(BF16)
-
+    out_x[edge:sites - edge, :] = own[edge:sites - edge].astype(BF16)
+    out_x[:edge, :] = (own[:edge] + grecv[1].astype(F32)).astype(BF16)
+    out_x[sites - edge:, :] = (own[sites - edge:sites] + grecv[0].astype(F32)).astype(BF16)
     x_out = pltpu.make_async_copy(out_x, to_x, lsem.at[5])
     x_out.start()
 
-    loss_step(4)
-    for s in (0, 2, 1, 3):
-        after_y(s)
-    loss_step(5)
-    loss_step(6)
-    loss_step(7)
+    for ahead in (2, 1, 3, 0):
+        after_y(ahead)
+    stages[1][1]()
+    stages[2][0]()
 
     total = s2[z // z4, z % z4].astype(F32)
     if comm:
@@ -273,8 +289,10 @@
     for u in range(1, n_space):
         copy = remote(ag.at[sp], ag.at[sp], ag_s.at[u], ag_r.at[u], sp_peer(u))
         start(copy)
-    loss_step(8)
-    loss_total = jnp.sum(lsum[len(chain)])
+    stages[2][1]()
+    stages[3][0]()
+    stages[3][1]()
+    loss_total = jnp.sum(lsum[4])
     out_loss[0, 0] = 0.5 * loss_total / (outs * total_count.astype(F32))
     if comm:
         for u in range(1, n_space):
@@ -295,7 +313,8 @@
     w_out.wait()
 
 
-def finish(x_in, w_in, x_out, w_out, x_v, w_v, sem):
+def finish(x_in, w_in, l_in, x_out, w_out, l_out, x_v, w_v, sem):
+    l_out[0, 0] = l_in[0, 0]
     first = [pltpu.make_async_copy(x_in, x_v, sem.at[0]), pltpu.make_async_copy(w_in, w_v, sem.at[1])]
     second = [pltpu.make_async_copy(x_v, x_out, sem.at[2]), pltpu.make_async_copy(w_v, w_out, sem.at[3])]
     for copy in first:
@@ -317,7 +336,7 @@
     z4 = nz // 4
     rows = offsets * chans // n_dp
     assert 48 < rows <= 64 and n_space == 8 and outs == 256 and chans == 128
-    n_loss = 5 + (nz - 1).bit_length()
+    n_loss = nz + 10
     tile = (16, 128)
     dma = pltpu.SemaphoreType.DMA
     results = (
@@ -357,7 +376,7 @@
             pltpu.VMEM((8,) + tile, F32),
             pltpu.VMEM((2, edge, chans), BF16),
             pltpu.VMEM((2, edge, chans), BF16),
-            pltpu.VMEM((n_loss + 1, 8, 128), F32),
+            pltpu.VMEM((5, 8, 128), F32),
             pltpu.VMEM((n_loss, 8, 128), F32),
             pltpu.SemaphoreType.REGULAR((3,)),
             dma((7,)), dma((2,)), dma((2,)), dma((4,)), dma((4,)), dma((2, 4, 4)), dma((2, 4, 4)),
@@ -369,12 +388,13 @@
             **(dict(collective_id=0, has_side_effects=True) if comm else {})),
     )(features, teacher, weight, neighbours.T, counts.reshape(-1, 128))
     anywhere = [pl.BlockSpec(memory_space=pl.ANY)] * 2
-    grad_x, grad_w = pl.pallas_call(
-        finish, out_shape=results[:2], in_specs=anywhere, out_specs=tuple(anywhere),
+    scalar = [pl.BlockSpec(memory_space=pltpu.SMEM)]
+    grad_x, grad_w, loss = pl.pallas_call(
+        finish, out_shape=results, in_specs=anywhere + scalar, out_specs=tuple(anywhere + scalar),
         scratch_shapes=[pltpu.VMEM((sites, chans), BF16), pltpu.VMEM((rows, outs), F32), dma((4,))],
         compiler_params=pltpu.CompilerParams(vmem_limit_bytes=56 * 1024 * 1024),
-    )(*done[:2])
-    return grad_x, grad_w, done[2].reshape(())
+    )(*done)
+    return grad_x, grad_w, loss.reshape(())
 
 
 def solution(mesh, comm=True):

time: 60.1 us -> 49.5 us (0.82)
  the two profiles are of different devices: /device:TPU:4 before, /device:TPU:2 now
where the time goes in v3:
time: 49.5 us; the launch traced here: 49.3 us
  Pallas kernels  48.7 us (98%)
  between operations  0.64 us (1%)
    pallas_call x1, Pallas kernels, shards(): pl.pallas_call(functools.partial(body, n_dp, n_space, comm), out_shape=re...  46 us
    pallas_call x1, Pallas kernels, shards(): pl.pallas_call(finish, out_shape=results, in_specs=anywhere + scalar, out...  2.66 us

profile of v3, /device:TPU:2, one launch (start us, length us, event | category | flops | bytes accessed | tf_op | source)
XLA Modules:
  0.0 49.3 jit_solution(11275308356081511334)
XLA Ops:
  0.6 46.0 %shard_map.76 = (bf16[256,128]{1,0:T(8,128)(2,1)}, f32[54,256]{1,0:T(8,128)}, f32[1,1]{1,0:T(1,128)}) custom-call(bf16[256,128]{1,0:T(8,128)(2,1)} %feats.1, bf16[256,256]{1,0:T(8,128)(2,1)} %teacher.1, bf16[3456,256]{1,0:T(8,128)(2,1)} %weight.1, s32[27,256]{1,0:T(8,128)} %bitcast.3, s32[4,128]{1,0:T(4,128)} %bitcast.4), custom_call_target="tpu_custom_call" | custom-call | tf_op jit(solution)/shard_map/pallas_call | solution.py:347
  46.7 2.7 %shard_map.77 = (bf16[256,128]{1,0:T(8,128)(2,1)}, f32[54,256]{1,0:T(8,128)}, f32[1,1]{1,0:T(1,128)}) custom-call(bf16[256,128]{1,0:T(8,128)(2,1)} %get-tuple-element.9.x_in, f32[54,256]{1,0:T(8,128)} %get-tuple-element.10.w_in, f32[1,1]{1,0:T(1,128)} %get-tuple-element.11.l_in), custom_call_target="tpu_custom_call" | custom-call | tf_op jit(solution)/shard_map/pallas_call | solution.py:392

commit v4 on v3

--- a/solution.py
+++ b/solution.py
@@ -22,10 +22,10 @@
 
 
 def body(n_dp, n_space, comm, feats, teacher, weight, nbrs, counts,
-         to_x, to_w, out_loss,
-         out_x, out_w,
-         win, nbr_v, count_v, teach_v, w_v, w_t, hot, g_t, gw, part, rc, s0, r1, s1, r2, s2,
-         rz, ag, gsend, grecv, lsum, lrecv,
+         to_x, ag, to_loss,
+         out_x, out_w, out_loss,
+         win, nbr_v, count_v, teach_v, w_v, w_t, hot, hot_edge, g_t, gw, part, rc, s0, r1, s1, r2, s2,
+         rz, gsend, grecv, lsum, lrecv,
          greeted, lsem, halo_s, halo_r, core_s, core_r, ring_s, ring_r, z_s, z_r, ag_s, ag_r, gh_s, gh_r, loss_s, loss_r):
     sites, chans = feats.shape
     outs = teacher.shape[1]
@@ -116,7 +116,9 @@
                       jnp.where((nbr_t >= 0) & (nbr_t < edge), nbr_t + sites, nbr_t))
     slot = lax.broadcasted_iota(jnp.int32, (slots, sites), 0)
     for k in range(offsets):
-        hot[k] = (slot == nbr_t[k:k + 1, :]).astype(F32).astype(BF16)
+        one = (slot == nbr_t[k:k + 1, :]).astype(F32).astype(BF16)
+        hot[k] = one[:sites]
+        hot_edge[k] = one[sites:]
 
     eye = (lax.broadcasted_iota(jnp.int32, (outs, outs), 0) == lax.broadcasted_iota(jnp.int32, (outs, outs), 1))
     eye = eye.astype(F32).astype(BF16)
@@ -135,13 +137,17 @@
 
     own_t = dot_nt(eye[:chans, :chans], win[:sites, :]).astype(BF16)
     for k in range(offsets):
-        g_t[k * chans:(k + 1) * chans, :] = dot(own_t, hot[k, :sites, :]).astype(BF16)
+        g_t[k * chans:(k + 1) * chans, :] = dot(own_t, hot[k]).astype(BF16)
     got(halo_up)
     got(halo_dn)
     edge_t = dot_nt(eye[:chans, :chans], win[sites:, :]).astype(BF16)
-    for k in range(offsets):
-        at = slice(k * chans, (k + 1) * chans)
-        g_t[at, :] = (g_t[at, :].astype(F32) + dot(edge_t, hot[k, sites:, :])).astype(BF16)
+    blank = jnp.zeros((chans, 2 * edge), BF16)
+    edge_2 = jnp.concatenate([jnp.concatenate([edge_t, blank], axis=1), jnp.concatenate([blank, edge_t], axis=1)], axis=0)
+    for k in range(0, offsets, 2):
+        n = min(2, offsets - k)
+        at = slice(k * chans, (k + n) * chans)
+        pair = hot_edge[k:k + n].reshape(n * 2 * edge, sites)
+        g_t[at, :] = (g_t[at, :].astype(F32) + dot(edge_2[:n * chans, :n * 2 * edge], pair)).astype(BF16)
     greetings(0)
     z_t = dot(w_t[...], g_t[...])
     at = lax.broadcasted_iota(jnp.int32, (outs, sites), 1)
@@ -180,7 +186,7 @@
     def ring(s, level):
         return (x, x_peer) if (s < 2) == (level == 0) else (y, y_peer)
 
-    steps = (1, 3, 2)
+    steps = (2, 1, 3)
     ring_copies = [[[remote((s0, s1)[level].at[s, (ring(s, level)[0] + t) % 4], (r1, r2)[level].at[s, t],
                             ring_s.at[level, s, t], ring_r.at[level, s, t], ring(s, level)[1](t))
                      for t in steps] for s in range(4)] for level in range(2)]
@@ -222,39 +228,46 @@
                     remote(s2.at[s, j], rz.at[back], z_s.at[back], z_r.at[back], z_peer(to)).start()
 
     block = 2 * z4 * rows
-    gw[:, block:, :] = jnp.zeros((2, gw.shape[1] - block, outs), F32)
+    gw[:, block:, :] = jnp.zeros((8, gw.shape[1] - block, outs), F32)
+    order = [(s, h) for s in (0, 2, 1, 3) for h in range(2)]
+
+    def product(s, h):
+        base = (h * 4 + s) * block
+        gw[h * 4 + s, :block, :] = dot_nt(g_t[base:base + block, :], dz_t)
+
+    product(*order[0])
     before = None
-    for s in (0, 2, 1, 3):
-        for h in range(2):
-            base = (h * 4 + s) * block
-            gw[h, :block, :] = dot_nt(g_t[base:base + block, :], dz_t)
-            for j in range(z4):
-                for c in range(2):
-                    frame = gw[h, (j * 2 + c) * rows:(j * 2 + c) * rows + 64, :].astype(BF16)
-                    for l in range(2):
-                        for q in range(4):
-                            at = (2 * h + l, q) if s < 2 else (q, 2 * h + l)
-                            part[c, s, at[0], at[1], j] = frame[16 * q:16 * q + 16, 128 * l:128 * l + 128]
-        start(core_copies[s])
-        if before is not None:
-            after_core(before)
-        before = s
-        if s == 1:
-            greetings(1)
+    for i, (s, h) in enumerate(order):
+        if i + 1 < len(order):
+            product(*order[i + 1])
+        for j in range(z4):
+            for c in range(2):
+                frame = gw[h * 4 + s, (j * 2 + c) * rows:(j * 2 + c) * rows + 64, :].astype(BF16)
+                for l in range(2):
+                    for q in range(4):
+                        at = (2 * h + l, q) if s < 2 else (q, 2 * h + l)
+                        part[c, s, at[0], at[1], j] = frame[16 * q:16 * q + 16, 128 * l:128 * l + 128]
+        if h == 1:
+            start(core_copies[s])
+            if before is not None:
+                after_core(before)
+            before = s
+            if s == 1:
+                greetings(1)
     after_core(before)
     greetings(2)
     stages[0][0]()
 
-    def spread_part(first, last, acc):
-        for k in range(first, last):
-            d_t = dot(w_v[k * chans:(k + 1) * chans, :], dz_t).astype(BF16)
-            acc = acc + dot_nt(d_t, hot[k])
-        return acc
-
-    spread = spread_part(0, offsets, jnp.zeros((chans, slots), F32))
+    spread = jnp.zeros((chans, sites), F32)
+    spread_edge = jnp.zeros((chans, 2 * edge), F32)
+    for k in range(offsets):
+        d_t = dot(w_v[k * chans:(k + 1) * chans, :], dz_t).astype(BF16)
+        spread = spread + dot_nt(d_t, hot[k])
+        spread_edge = spread_edge + dot_nt(d_t, hot_edge[k])
     own = jnp.transpose(spread)
-    gsend[0] = own[sites:sites + edge].astype(BF16)
-    gsend[1] = own[sites + edge:].astype(BF16)
+    away = jnp.transpose(spread_edge)
+    gsend[0] = away[:edge].astype(BF16)
+    gsend[1] = away[edge:].astype(BF16)
     gh_dn = remote(gsend.at[0], grecv.at[0], gh_s.at[0], gh_r.at[0], sp_peer(n_space - 1))
     gh_up = remote(gsend.at[1], grecv.at[1], gh_s.at[1], gh_r.at[1], sp_peer(1))
     start(gh_dn)
@@ -284,26 +297,22 @@
             incoming = remote(rz.at[t], rz.at[t], z_s.at[t], z_r.at[t], z_peer(z))
             incoming.wait_recv()
             total = total + rz[t].astype(F32)
-    ag[sp] = total
-    ag_copies = []
-    for u in range(1, n_space):
-        copy = remote(ag.at[sp], ag.at[sp], ag_s.at[u], ag_r.at[u], sp_peer(u))
-        start(copy)
+    out_w[...] = total
+    w_out = pltpu.make_async_copy(out_w, ag.at[sp], lsem.at[6])
+    w_out.start()
+    for u in (6, 2, 3, 5, 4, 1, 7):
+        start(remote(out_w, ag.at[sp], ag_s.at[u], ag_r.at[u], sp_peer(u)))
     stages[2][1]()
     stages[3][0]()
     stages[3][1]()
-    loss_total = jnp.sum(lsum[4])
-    out_loss[0, 0] = 0.5 * loss_total / (outs * total_count.astype(F32))
+    loss_total = jnp.sum(lsum[4], keepdims=True)
+    out_loss[...] = 0.5 * loss_total / (outs * total_count.astype(F32))
+    l_out = pltpu.make_async_copy(out_loss, to_loss, lsem.at[7])
+    l_out.start()
     if comm:
         for u in range(1, n_space):
             source = (sp - u + n_space) % n_space
-            remote(ag.at[source], ag.at[source], ag_s.at[u], ag_r.at[u], sp_peer(u)).wait_recv()
-    for p in range(8):
-        q, h = p % 4, p // 4
-        keep = min(16, rows - 16 * q)
-        out_w[16 * q:16 * q + keep, 128 * h:128 * h + 128] = ag[p][:keep]
-    w_out = pltpu.make_async_copy(out_w, to_w, lsem.at[6])
-    w_out.start()
+            remote(out_w, ag.at[source], ag_s.at[u], ag_r.at[u], sp_peer(u)).wait_recv()
     for copy in sent:
         copy.wait_send()
     if comm:
@@ -311,17 +320,25 @@
             remote(rz.at[t], rz.at[t], z_s.at[t], z_r.at[t], z_peer(z)).wait_send()
     x_out.wait()
     w_out.wait()
-
-
-def finish(x_in, w_in, l_in, x_out, w_out, l_out, x_v, w_v, sem):
-    l_out[0, 0] = l_in[0, 0]
-    first = [pltpu.make_async_copy(x_in, x_v, sem.at[0]), pltpu.make_async_copy(w_in, w_v, sem.at[1])]
-    second = [pltpu.make_async_copy(x_v, x_out, sem.at[2]), pltpu.make_async_copy(w_v, w_out, sem.at[3])]
+    l_out.wait()
+
+
+def finish(x_in, pieces_in, l_in, x_out, w_out, l_out, x_v, pieces, w_v, l_v, sem):
+    first = [pltpu.make_async_copy(a, b, sem.at[i])
+             for i, (a, b) in enumerate(((x_in, x_v), (l_in, l_v), (pieces_in, pieces)))]
+    second = [pltpu.make_async_copy(a, b, sem.at[3 + i])
+              for i, (a, b) in enumerate(((x_v, x_out), (l_v, l_out), (w_v, w_out)))]
     for copy in first:
         copy.start()
-    for copy, then in zip(first, second):
-        copy.wait()
-        then.start()
+    for i in range(2):
+        first[i].wait()
+        second[i].start()
+    first[2].wait()
+    for p in range(8):
+        q, h = p % 4, p // 4
+        keep = min(16, w_v.shape[0] - 16 * q)
+        w_v[16 * q:16 * q + keep, 128 * h:128 * h + 128] = pieces[p][:keep]
+    second[2].start()
     for copy in second:
         copy.wait()
 
@@ -346,25 +363,27 @@
     )
     done = pl.pallas_call(
         functools.partial(body, n_dp, n_space, comm),
-        out_shape=results,
+        out_shape=(results[0], jax.ShapeDtypeStruct((8,) + tile, F32), results[2]),
         in_specs=[pl.BlockSpec(memory_space=pl.ANY)] * 5,
         out_specs=(
             pl.BlockSpec(memory_space=pl.ANY),
             pl.BlockSpec(memory_space=pl.ANY),
-            pl.BlockSpec(memory_space=pltpu.SMEM),
+            pl.BlockSpec(memory_space=pl.ANY),
         ),
         scratch_shapes=[
             pltpu.VMEM((sites, chans), BF16),
-            pltpu.VMEM((rows, outs), F32),
+            pltpu.VMEM(tile, F32),
+            pltpu.VMEM((1, 1), F32),
             pltpu.VMEM((slots, chans), BF16),
             pltpu.VMEM((offsets, sites), jnp.int32),
             pltpu.VMEM((n_dp * n_space // 128, 128), jnp.int32),
             pltpu.VMEM((sites, outs), BF16),
             pltpu.VMEM((offsets * chans, outs), BF16),
             pltpu.VMEM((outs, offsets * chans), BF16),
-            pltpu.VMEM((offsets, slots, sites), BF16),
+            pltpu.VMEM((offsets, sites, sites), BF16),
+            pltpu.VMEM((offsets, 2 * edge, sites), BF16),
             pltpu.VMEM((offsets * chans, sites), BF16),
-            pltpu.VMEM((2, 2 * z4 * rows + 16, outs), F32),
+            pltpu.VMEM((8, 2 * z4 * rows + 16, outs), F32),
             pltpu.VMEM((2, 4, 4, 4, z4) + tile, BF16),
             pltpu.VMEM((4, 4, 4, z4) + tile, BF16),
             pltpu.VMEM((4, 4, 4, z4) + tile, BF16),
@@ -373,13 +392,12 @@
             pltpu.VMEM((4, 4, z4) + tile, BF16),
             pltpu.VMEM((4, z4) + tile, BF16),
             pltpu.VMEM((nz,) + tile, BF16),
-            pltpu.VMEM((8,) + tile, F32),
             pltpu.VMEM((2, edge, chans), BF16),
             pltpu.VMEM((2, edge, chans), BF16),
             pltpu.VMEM((5, 8, 128), F32),
             pltpu.VMEM((n_loss, 8, 128), F32),
             pltpu.SemaphoreType.REGULAR((3,)),
-            dma((7,)), dma((2,)), dma((2,)), dma((4,)), dma((4,)), dma((2, 4, 4)), dma((2, 4, 4)),
+            dma((8,)), dma((2,)), dma((2,)), dma((4,)), dma((4,)), dma((2, 4, 4)), dma((2, 4, 4)),
             dma((nz,)), dma((nz,)), dma((n_space,)), dma((n_space,)), dma((2,)), dma((2,)),
             dma((n_loss,)), dma((n_loss,)),
         ],
@@ -387,11 +405,11 @@
             vmem_limit_bytes=56 * 1024 * 1024,
             **(dict(collective_id=0, has_side_effects=True) if comm else {})),
     )(features, teacher, weight, neighbours.T, counts.reshape(-1, 128))
-    anywhere = [pl.BlockSpec(memory_space=pl.ANY)] * 2
-    scalar = [pl.BlockSpec(memory_space=pltpu.SMEM)]
+    anywhere = [pl.BlockSpec(memory_space=pl.ANY)] * 3
     grad_x, grad_w, loss = pl.pallas_call(
-        finish, out_shape=results, in_specs=anywhere + scalar, out_specs=tuple(anywhere + scalar),
-        scratch_shapes=[pltpu.VMEM((sites, chans), BF16), pltpu.VMEM((rows, outs), F32), dma((4,))],
+        finish, out_shape=results, in_specs=anywhere, out_specs=tuple(anywhere),
+        scratch_shapes=[pltpu.VMEM((sites, chans), BF16), pltpu.VMEM((8,) + tile, F32), pltpu.VMEM((rows, outs), F32),
+                        pltpu.VMEM((1, 1), F32), dma((6,))],
         compiler_params=pltpu.CompilerParams(vmem_limit_bytes=56 * 1024 * 1024),
     )(*done)
     return grad_x, grad_w, loss.reshape(())

time: 49.5 us -> 48.1 us (0.972)
  Pallas kernels: 48.7 us -> 47.3 us
    pallas_call x2, Pallas kernels: 48.7 us -> 47.3 us  [the longest x1 45.1 us: shards(): pl.pallas_call(functools.partial(body, n_dp, n_space, comm), out_shape=(r...]
where the time goes in v4:
time: 48.1 us; the launch traced here: 47.9 us
  Pallas kernels  47.3 us (98%)
  between operations  0.64 us (1%)
    pallas_call x1, Pallas kernels, shards(): pl.pallas_call(functools.partial(body, n_dp, n_space, comm), out_shape=(r...  45.1 us
    pallas_call x1, Pallas kernels, shards(): pl.pallas_call(finish, out_shape=results, in_specs=anywhere, out_specs=tu...  2.17 us

profile of v4, /device:TPU:2, one launch (start us, length us, event | category | flops | bytes accessed | tf_op | source)
XLA Modules:
  0.0 47.9 jit_solution(10116940790543029239)
XLA Ops:
  0.6 45.1 %shard_map.76 = (bf16[256,128]{1,0:T(8,128)(2,1)}, f32[8,16,128]{2,1,0:T(8,128)}, f32[1,1]{1,0:T(1,128)}) custom-call(bf16[256,128]{1,0:T(8,128)(2,1)} %feats.1, bf16[256,256]{1,0:T(8,128)(2,1)} %teacher.1, bf16[3456,256]{1,0:T(8,128)(2,1)} %weight.1, s32[27,256]{1,0:T(8,128)} %bitcast.3, s32[4,128]{1,0:T(4,128)} %bitcast.4), custom_call_target="tpu_custom_call" | custom-call | tf_op jit(solution)/shard_map/pallas_call | solution.py:364
  45.7 2.2 %shard_map.77 = (bf16[256,128]{1,0:T(8,128)(2,1)}, f32[54,256]{1,0:T(8,128)}, f32[1,1]{1,0:T(1,128)}) custom-call(bf16[256,128]{1,0:T(8,128)(2,1)} %get-tuple-element.9.x_in, f32[8,16,128]{2,1,0:T(8,128)} %get-tuple-element.10.pieces_in, f32[1,1]{1,0:T(1,128)} %get-tuple-element.11.l_in), custom_call_target="tpu_custom_call" | custom-call | tf_op jit(solution)/shard_map/pallas_call | solution.py:409

commit v5 on v4

--- a/solution.py
+++ b/solution.py
@@ -258,10 +258,11 @@
     greetings(2)
     stages[0][0]()
 
+    g_t[...] = dot(w_v[...], dz_t).astype(BF16)
     spread = jnp.zeros((chans, sites), F32)
     spread_edge = jnp.zeros((chans, 2 * edge), F32)
     for k in range(offsets):
-        d_t = dot(w_v[k * chans:(k + 1) * chans, :], dz_t).astype(BF16)
+        d_t = g_t[k * chans:(k + 1) * chans, :]
         spread = spread + dot_nt(d_t, hot[k])
         spread_edge = spread_edge + dot_nt(d_t, hot_edge[k])
     own = jnp.transpose(spread)

time: 48.1 us -> 47.6 us (0.990)
  Pallas kernels: 47.3 us -> 46.8 us
    pallas_call x1, Pallas kernels: 45.1 us -> 44.6 us  [shards(): pl.pallas_call(functools.partial(body, n_dp, n_space, comm), out_shape=(r...]
where the time goes in v5:
time: 47.6 us; the launch traced here: 47.4 us
  Pallas kernels  46.8 us (98%)
  between operations  0.64 us (1%)
    pallas_call x1, Pallas kernels, shards(): pl.pallas_call(functools.partial(body, n_dp, n_space, comm), out_shape=(r...  44.6 us
    pallas_call x1, Pallas kernels, shards(): pl.pallas_call(finish, out_shape=results, in_specs=anywhere, out_specs=tu...  2.17 us

profile of v5, /device:TPU:2, one launch (start us, length us, event | category | flops | bytes accessed | tf_op | source)
XLA Modules:
  0.0 47.4 jit_solution(7833493189795794717)
XLA Ops:
  0.6 44.6 %shard_map.76 = (bf16[256,128]{1,0:T(8,128)(2,1)}, f32[8,16,128]{2,1,0:T(8,128)}, f32[1,1]{1,0:T(1,128)}) custom-call(bf16[256,128]{1,0:T(8,128)(2,1)} %feats.1, bf16[256,256]{1,0:T(8,128)(2,1)} %teacher.1, bf16[3456,256]{1,0:T(8,128)(2,1)} %weight.1, s32[27,256]{1,0:T(8,128)} %bitcast.3, s32[4,128]{1,0:T(4,128)} %bitcast.4), custom_call_target="tpu_custom_call" | custom-call | tf_op jit(solution)/shard_map/pallas_call | solution.py:365
  45.2 2.2 %shard_map.77 = (bf16[256,128]{1,0:T(8,128)(2,1)}, f32[54,256]{1,0:T(8,128)}, f32[1,1]{1,0:T(1,128)}) custom-call(bf16[256,128]{1,0:T(8,128)(2,1)} %get-tuple-element.9.x_in, f32[8,16,128]{2,1,0:T(8,128)} %get-tuple-element.10.pieces_in, f32[1,1]{1,0:T(1,128)} %get-tuple-element.11.l_in), custom_call_target="tpu_custom_call" | custom-call | tf_op jit(solution)/shard_map/pallas_call | solution.py:410
